TPU v7x, 32 devices: a whole 2x2x4 slice. The times are simulated.
32 devices in a mesh: mode: 8 (over z, x), slab: 4 (over y, core).
Axes of the slice: x: 2, y: 2, z: 4, core: 2. Of those that a mesh axis runs over, the one named last changes fastest.
Arguments:
- field: float32 [128, 16, 64, 128], P('mode', 'slab'), may hold values from -6 to 6
- coefficient_fields: float32 [16, 16, 64, 128], P(None, 'slab', 'mode'), may hold values from -6 to 6
- triple_blocks: float32 [16, 4, 32, 64], replicated, may hold values from -0.1875 to 0.1875
- block_pattern: int32 [16, 4, 2], replicated, may hold values from 0 to 3
Outputs:
- result: float32 [128, 16, 64, 128], P('mode', 'slab')
All inputs are finite; a program needn't handle non-finite values.
Results may differ from a plain program's by a relative error of at most 0.0003.
Values sent between devices are 32-bit elements; how exact they have to be, the bound alone decides.
No kernel may reach another device: no remote copies, remote signals or barrier semaphores. Data moves between devices by JAX's collectives and lax.ppermute only.
A program may use at most 128 MiB of HBM per device.

v0:
```python
import functools

import jax
import jax.numpy as jnp
from jax import lax
from jax.experimental import pallas as pl
from jax.experimental.pallas import tpu as pltpu
from jax.sharding import PartitionSpec as P

F32 = jnp.float32
BF16 = jnp.bfloat16
VMEM = pl.BlockSpec(memory_space=pltpu.VMEM)
SMEM = pl.BlockSpec(memory_space=pltpu.SMEM)
MIB = 2**20


def params(mib):
    return pltpu.CompilerParams(vmem_limit_bytes=mib * MIB)


def cost(flops, size):
    return pl.CostEstimate(flops=int(flops), bytes_accessed=int(size), transcendentals=0)


def from_behind(value, axis, steps):
    count = lax.axis_size(axis)
    first, last = (max(0, -steps), min(count, count - steps))
    return lax.ppermute(value, axis, [(source, source + steps) for source in range(first, last)])


def exchange(pieces, order):
    count = len(pieces)
    received = list(pieces)
    for s in order:
        received[s] = lax.ppermute(pieces[s], "mode", [(i, i ^ s) for i in range(count)])
    return received


def part_of(owner, size):
    return pl.ds(pl.multiple_of(owner * size, size), size)


def after(owner, count):
    return jnp.minimum(owner + 1, count - 1)


def split(value):
    high = value.astype(BF16)
    return high, (value - high.astype(F32)).astype(BF16)


def prepare_kernel(count, me_ref, pattern_ref, blocks_ref, field_ref, *outs):
    dense_refs, weights_ref = outs[:4], outs[4]
    fields, row_blocks, block, stored = blocks_ref.shape
    modes = row_blocks * block
    half = modes // 2
    lane = lax.broadcasted_iota(jnp.int32, (block, modes), 1)
    side = me_ref[0] // (count // 2)

    def one_field(k, carry):
        for j in range(row_blocks):
            rows_side, local = divmod(j, row_blocks // 2)
            r = (side ^ rows_side) * (row_blocks // 2) + local
            value = blocks_ref[k, r]
            value = jnp.concatenate([value, jnp.zeros((block, modes - stored), F32)], axis=1)
            total = None
            for c in range(stored // block):
                part = jnp.where((lane >= c * block) & (lane < (c + 1) * block), value, 0.0)
                shift = lax.rem(pattern_ref[k, r, c] - c + row_blocks, row_blocks) * block
                part = pltpu.roll(part, shift, 1)
                total = part if total is None else total + part
            total = pltpu.roll(total, side * half, 1)
            high, low = (part.astype(F32) for part in split(total))
            other_high, other_low = pltpu.roll(high, half, 1), pltpu.roll(low, half, 1)
            rows = pl.ds(pl.multiple_of(k * half + local * block, block), block)
            near = jnp.where(lane < half, high, other_low).astype(BF16), high[:, :half].astype(BF16)
            far = jnp.where(lane < half, other_high, low).astype(BF16), other_high[:, :half].astype(BF16)
            for columns_side, parts in enumerate((near, far)):
                dense_refs[2 * columns_side + rows_side][rows, 0:modes] = parts[0]
                dense_refs[2 * columns_side + rows_side][rows, modes:] = parts[1]
        return carry

    lax.fori_loop(0, fields, one_field, 0)
    for z in range(weights_ref.shape[0]):
        weights_ref[z] = jnp.swapaxes(field_ref[:, z], 0, 1)


def prepare(me, triple_blocks, block_pattern, coefficient_fields, count):
    fields, row_blocks, block, _ = triple_blocks.shape
    modes = row_blocks * block
    _, depth, rows, width = coefficient_fields.shape
    part = jax.ShapeDtypeStruct((fields * modes // 2, 3 * modes // 2), BF16)
    *parts, weights = pl.pallas_call(
        functools.partial(prepare_kernel, count),
        in_specs=[SMEM, SMEM, VMEM, VMEM],
        out_specs=[VMEM] * 5,
        out_shape=[part] * 4 + [jax.ShapeDtypeStruct((depth, rows, fields, width), F32)],
        compiler_params=params(16),
        cost_estimate=cost(1, 1),
        name="prepare",
    )(me, block_pattern, triple_blocks, coefficient_fields)
    return {(i // 2, i % 2): part for i, part in enumerate(parts)}, weights


def pack_kernel(count, me_ref, field_ref, *outs):
    me = me_ref[0]
    rows = field_ref.shape[2] // count
    for s, out in enumerate(outs):
        owner = me ^ s
        own = field_ref[:, 0, part_of(owner, rows), :]
        out[0, :rows] = jnp.swapaxes(own, 0, 1)
        ahead = field_ref[:, 0, part_of(after(owner, count), rows), :][:, 0]
        out[0, rows] = jnp.where(owner < count - 1, ahead, 0.0)


def pack(me, field, count):
    modes, depth, height, width = field.shape
    rows = height // count
    block = (1, rows + 1, modes, width)
    return pl.pallas_call(
        functools.partial(pack_kernel, count),
        grid=(depth,),
        in_specs=[SMEM, pl.BlockSpec((modes, 1, height, width), lambda i: (0, i, 0, 0))],
        out_specs=[pl.BlockSpec(block, lambda i: (i, 0, 0, 0))] * count,
        out_shape=[jax.ShapeDtypeStruct((depth,) + block[1:], F32)] * count,
        compiler_params=params(16),
        cost_estimate=cost(1, 1),
        name="pack",
    )(me, field)


def half_row(me, s, count, size):
    return part_of((me ^ s) & (count // 2 - 1), size)


def ahead_x(value):
    width = value.shape[-1]
    lane = lax.broadcasted_iota(jnp.int32, value.shape, 1)
    return jnp.where(lane == width - 1, 0.0, pltpu.roll(value, width - 1, 1))


def behind_x(value):
    lane = lax.broadcasted_iota(jnp.int32, value.shape, 1)
    return jnp.where(lane == 0, 0.0, pltpu.roll(value, 1, 1))


def edges_kernel(count, picks, me_ref, *refs):
    me = me_ref[0]
    near, far, outs = refs[: len(picks)], refs[len(picks) : len(picks) + count // 2], refs[len(picks) + count // 2 :]
    for out, own, index in zip(outs, near, picks):
        rows, modes, _ = out.shape
        out[:, : modes // 2, :] = own[...]
        for i, ref in enumerate(far):
            size = ref.shape[2]
            start = modes // 2 + ((me ^ (i + count // 2)) & (count // 2 - 1)) * size
            out[:, pl.ds(pl.multiple_of(start, size), size), :] = ref[index, :rows]


def edges(me, near, far, picks, count):
    rows, half, width = near[0].shape
    return pl.pallas_call(
        functools.partial(edges_kernel, count, picks),
        in_specs=[SMEM] + [VMEM] * (len(near) + len(far)),
        out_specs=[VMEM] * len(picks),
        out_shape=[jax.ShapeDtypeStruct((rows, 2 * half, width), F32)] * len(picks),
        compiler_params=params(16),
        cost_estimate=cost(1, 1),
        name="edges",
    )(me, *near, *far)


def couple(c_refs, rhs_ref, groups, weights, per_step):
    flat = [gradient for group in groups for gradient in group]
    owner = [r for r, group in enumerate(groups) for _ in group]
    half, width = flat[0].shape
    for i, gradient in enumerate(flat):
        high, low = split(gradient)
        lanes = slice(i * width, (i + 1) * width)
        rhs_ref[0:half, lanes] = high
        rhs_ref[half : 2 * half, lanes] = high
        rhs_ref[2 * half :, lanes] = low
    rhs = rhs_ref[:, : len(flat) * width]
    results = []
    for c_ref in c_refs:
        fields = c_ref.shape[0] // half
        totals = [None] * len(flat)
        for k0 in range(0, fields, per_step):
            product = jnp.dot(c_ref[k0 * half : (k0 + per_step) * half, :], rhs, preferred_element_type=F32)
            for k in range(per_step):
                for i in range(len(flat)):
                    part = product[k * half : (k + 1) * half, i * width : (i + 1) * width]
                    part = part * weights[owner[i]][k0 + k : k0 + k + 1, :]
                    totals[i] = part if totals[i] is None else totals[i] + part
        results.append(totals)
    return results


def flux_kernel(count, plan, me_ref, w_ref, *refs):
    tasks, dense_keys, sources, behind, sums_in, final, carried, edges = plan
    me = me_ref[0]
    refs = list(refs)
    dense = {key: refs.pop(0) for key in dense_keys}
    w_behind = refs.pop(0) if behind else None
    ins = [[refs.pop(0) for _ in range(number)] for _, _, number, _ in sources]
    sums = {key: refs.pop(0) for key in sums_in}
    outs = [refs.pop(0) for _ in range(count // 2 if final else 0)]
    total = {key: refs.pop(0) for key in carried}
    edge_refs = [refs.pop(0) for _ in edges]
    planes_ref, rhs_ref = refs.pop(0), refs.pop(0)
    for key in final:
        total[key] = refs.pop(0)
    _, full_rows, half_modes, width = planes_ref.shape
    rows = full_rows - 1
    slot = {}
    for (plane, half, _, index), group in zip(sources, ins):
        here = slot[plane, half] = len(slot)
        if len(group) == 1:
            planes_ref[here, :rows] = group[0][:, half * half_modes : (half + 1) * half_modes, :]
        else:
            for i, ref in enumerate(group):
                planes_ref[here, :, half_row(me, i + half * count // 2, count, ref.shape[2]), :] = ref[index]
    for ref, key in zip(edge_refs, edges):
        ref[...] = planes_ref[slot[key], :rows]
    for key, ref in total.items():
        ref[...] = sums[key][...] if key in sums else jnp.zeros_like(ref)

    for plane, directions, half, sides in tasks:
        per_step = 4 if len(directions) > 1 else 8

        def step(i, carry, plane=plane, directions=directions, half=half, sides=sides, per_step=per_step):
            groups, weights = [], []
            for j in range(per_step):
                y = per_step * i + j
                here = planes_ref[slot[plane, half], y]
                group = []
                if "x" in directions:
                    group.append(ahead_x(here) - here)
                if "y" in directions:
                    group.append(planes_ref[slot[plane, half], y + 1] - here)
                if "z" in directions:
                    group.append(planes_ref[slot[plane + 1, half], y] - here)
                groups.append(group)
                weights.append(w_behind[0, y] if plane < 0 else w_ref[plane, y])
            results = couple([dense[half, side] for side in sides], rhs_ref, groups, weights, 4)
            for side, fluxes in zip(sides, results):
                here = total.get((plane, side))
                above = total.get((plane + 1, side))
                for j in range(per_step):
                    y = per_step * i + j
                    change = None
                    for direction in directions:
                        flux = fluxes.pop(0)
                        part = behind_x(flux) - flux if direction == "x" else -flux
                        change = part if change is None else change + part
                        if direction == "y":
                            here[y + 1] += flux
                        if direction == "z" and above is not None:
                            above[y] += flux
                    if here is not None:
                        here[y] += change
            return carry

        lax.fori_loop(0, rows // per_step, step, 0)
    side = final[0][1] if final else 0
    for i, out in enumerate(outs):
        for z, key in enumerate(final):
            out[z] = total[key][:, half_row(me, i + side * count // 2, count, out.shape[2]), :]


def fluxes(me, dense, weights, behind, tasks, sources, sums, final, carried, count, edges=(), busy=True):
    _, rows, fields, width = weights.shape
    half_modes = dense[0, 0].shape[0] // fields
    dense_keys = tuple(sorted({(half, side) for _, _, half, sides in tasks for side in sides}))
    needed = {(p, h) for p, _, h, _ in tasks} | {(p + 1, h) for p, directions, h, _ in tasks if "z" in directions}
    needed = sorted(needed | set(edges))
    listed = tuple((p, h, len(sources[p, h][0]), sources[p, h][1]) for p, h in needed)
    plan = (tasks, dense_keys, listed, behind is not None, tuple(sums), final, carried, edges)
    args = [weights] + [dense[key] for key in dense_keys] + ([] if behind is None else [behind])
    args += [array for key in needed for array in sources[key][0]] + list(sums.values())
    whole = (rows + 1, half_modes, width)
    piece = jax.ShapeDtypeStruct((len(final), rows + 1, 2 * half_modes // count, width), F32)
    out_shape = [piece] * (count // 2 if final else 0)
    number_out = len(out_shape)
    out_shape += [jax.ShapeDtypeStruct(whole, F32)] * len(carried)
    out_shape += [jax.ShapeDtypeStruct((rows, half_modes, width), F32)] * len(edges)
    scratch = [pltpu.VMEM((len(listed),) + whole, F32), pltpu.VMEM((3 * half_modes, 12 * width), BF16)]
    scratch += [pltpu.VMEM(whole, F32)] * len(final)
    units = rows * sum(len(directions) * len(sides) for _, directions, _, sides in tasks)
    results = pl.pallas_call(
        functools.partial(flux_kernel, count, plan),
        in_specs=[SMEM] + [VMEM] * len(args),
        out_specs=[VMEM] * len(out_shape),
        out_shape=out_shape,
        scratch_shapes=scratch,
        compiler_params=params(32),
        cost_estimate=cost(busy * units * 4 * dense[0, 0].shape[0] * 2 * half_modes * width, 1),
        name="fluxes_" + "_".join(f"{p}{directions}{half}" for p, directions, half, _ in tasks),
    )(me, *args)
    sums_out = dict(zip(carried, results[number_out:]))
    return results[:number_out], sums_out, results[number_out + len(carried) :]


def unpack_kernel(count, chunks, me_ref, *refs):
    me = me_ref[0]
    step = pl.program_id(0)
    out = refs[-1]
    for c, planes in enumerate(chunks):
        chosen = functools.reduce(lambda left, right: left | right, [step == plane for plane in planes])

        @pl.when(chosen)
        def _(ins=refs[c * count : (c + 1) * count][::-1]):
            rows = ins[0].shape[1] - 1
            for s, ref in enumerate(ins):
                out[:, 0, part_of(me ^ s, rows), :] = jnp.swapaxes(ref[0, :rows], 0, 1)
            for s, ref in enumerate(ins):
                owner = me ^ s
                there = part_of(after(owner, count), rows)
                added = jnp.where(owner < count - 1, ref[0, rows], 0.0)[:, None, :]
                value = out[:, 0, there, :]
                row = lax.broadcasted_iota(jnp.int32, value.shape, 1)
                out[:, 0, there, :] = value + jnp.where(row == 0, added, 0.0)


def unpack(me, received, chunks, shape):
    modes, depth, height, width = shape
    count = len(received[0])
    in_specs, args = [SMEM], [me]
    for planes, pieces in zip(chunks, received):

        def place(i, planes=planes):
            return (functools.reduce(jnp.add, [(i >= plane).astype(jnp.int32) for plane in planes[1:]], 0), 0, 0, 0)

        in_specs += [pl.BlockSpec((1,) + pieces[0].shape[1:], place)] * count
        args += list(pieces)[::-1]
    return pl.pallas_call(
        functools.partial(unpack_kernel, count, chunks),
        grid=(depth,),
        in_specs=in_specs,
        out_specs=pl.BlockSpec((modes, 1, height, width), lambda i: (0, i, 0, 0)),
        out_shape=jax.ShapeDtypeStruct(shape, F32),
        compiler_params=params(16),
        cost_estimate=cost(1, 1),
        name="unpack",
    )(*args)


def body(field, coefficient_fields, triple_blocks, block_pattern):
    count = lax.axis_size("mode")
    depth = field.shape[1]
    top = depth - 1
    me = lax.axis_index("mode").astype(jnp.int32).reshape(1)
    near, far = tuple(range(1, count // 2)), tuple(range(count // 2, count))
    forth = far[:1] + near + far[1:]

    sent = exchange(pack(me, field, count), forth)
    dense, weights = prepare(me, triple_blocks, block_pattern, coefficient_fields, count)
    weights_behind = from_behind(weights[top:], "slab", 1)
    sides = (sent[: count // 2], sent[count // 2 :])
    sources = {(p, h): (sides[h], p) for p in range(depth) for h in (0, 1)}

    def add(*args, **options):
        return fluxes(me, dense, weights, *args, count, **options)

    def keys(side):
        return tuple((p, side) for p in range(depth))

    def inside(half, to):
        return tuple((p, "xyz", half, to) for p in range(top)) + ((top, "xy", half, to),)

    def outside(to):
        return tuple((p, "z", half, to) for half in (0, 1) for p in (top, -1))

    _, sums, near_ends = add(None, inside(0, (0, 1)), sources, {}, (), keys(0) + keys(1), edges=((0, 0), (top, 0)), busy=False)
    lowest, highest = edges(me, near_ends, sides[1], (0, top), count)
    above = from_behind(lowest, "slab", -1)
    below = from_behind(highest, "slab", 1)
    for half in (0, 1):
        sources[depth, half] = ([above], 0)
        sources[-1, half] = ([below], 0)
    _, far_sums, _ = add(None, inside(1, (1,)), sources, {key: sums[key] for key in keys(1)}, (), keys(1))
    far_pieces, _, _ = add(weights_behind, outside((1,)), sources, far_sums, keys(1), ())
    near_sums = {key: sums[key] for key in keys(0)}
    near_pieces, _, _ = add(weights_behind, inside(1, (0,)) + outside((0,)), sources, near_sums, keys(0), ())
    back = exchange(list(near_pieces) + list(far_pieces), far + near)
    return unpack(me, (back,), (tuple(range(depth)),), field.shape)


def solution(mesh):
    in_specs = (P("mode", "slab", None, None), P(None, "slab", "mode", None), P(), P())
    out_specs = P("mode", "slab", None, None)
    return jax.shard_map(body, mesh=mesh, in_specs=in_specs, out_specs=out_specs, check_vma=False)
```

profile of v0, /device:TPU:1, one launch (start us, length us, event | category | flops | bytes accessed | tf_op | source)
XLA Modules:
  0.0 134.6 jit_solution(8907175060372631008)
XLA Ops:
  0.0 1.6 %copy-done = f32[16,4,64,128]{3,2,1,0:T(8,128)S(1)} copy-done((f32[16,4,64,128]{3,2,1,0:T(8,128)S(1)}, f32[16,4,64,128]{3,2,1,0:T(8,128)}, u32[]{:S(2)}) %copy-start) | copy-done | bytes 2097176
  1.6 1.9 %pack.1 = (f32[4,9,16,128]{3,2,1,0:T(8,128)S(1)}, f32[4,9,16,128]{3,2,1,0:T(8,128)S(1)}, f32[4,9,16,128]{3,2,1,0:T(8,128)S(1)}, f32[4,9,16,128]{3,2,1,0:T(8,128)...) custom-call(s32[1]{0:T(128)} %bitcast.me_ref, ...), custom_call_target="tpu_custom_call" | custom-call | flops 1 | bytes 1 | tf_op jit(solution)/shard_map/pack/pallas_call | solution.py:120
  3.6 2.0 %collective-permute-start.1 = (f32[4,9,16,128]{3,2,1,0:T(8,128)S(1)}, f32[4,9,16,128]{3,2,1,0:T(8,128)S(1)}, u32[]{:S(2)}, u32[]{:S(2)}) collective-permute-start(f32[4,9,16,128]{3,2,1,0:T(8,128)S(1)} %get-tuple-element.47), channel_id=1, source_target_pairs={{0,4},{4,0},{8,12},{12,8},{16,20},{20,16},{24,28},{28,24},{1,5},{5... | collective-permute-start | bytes 884744 | tf_op jit(solution)/shard_map/ppermute | solution.py:35
  6.9 2.4 %collective-permute-start.4 = (f32[4,9,16,128]{3,2,1,0:T(8,128)}, f32[4,9,16,128]{3,2,1,0:T(8,128)S(1)}, u32[]{:S(2)}, u32[]{:S(2)}) collective-permute-start(f32[4,9,16,128]{3,2,1,0:T(8,128)} %get-tuple-element.52), channel_id=1, source_target_pairs={{0,16},{4,20},{8,24},{12,28},{16,0},{20,4},{24,8},{28,12},{1,17},{... | collective-permute-start | bytes 884744 | tf_op jit(solution)/shard_map/ppermute | solution.py:35
  10.3 2.0 %collective-permute-done.1.refs_3_.refs_7_.refs_11_.refs_15_.refs_6_.refs_14_.refs_22_ = f32[4,9,16,128]{3,2,1,0:T(8,128)S(1)} collective-permute-done((f32[4,9,16,128]{3,2,1,0:T(8,128)S(1)}, f32[4,9,16,128]{3,2,1,0:T(8,128)S(1)}, u32[]{:S(2)}, u32[]{:S(2)}) %collective-permute-start.1) | collective-permute-done | bytes 294944 | tf_op jit(solution)/shard_map/ppermute | solution.py:35
  12.3 3.3 %collective-permute-start.6 = (f32[4,9,16,128]{3,2,1,0:T(8,128)}, f32[4,9,16,128]{3,2,1,0:T(8,128)S(1)}, u32[]{:S(2)}, u32[]{:S(2)}) collective-permute-start(f32[4,9,16,128]{3,2,1,0:T(8,128)} %get-tuple-element.54), channel_id=1, source_target_pairs={{0,24},{4,28},{8,16},{12,20},{16,8},{20,12},{24,0},{28,4},{1,25},{... | collective-permute-start | bytes 884744 | tf_op jit(solution)/shard_map/ppermute | solution.py:35
  15.6 9.1 %collective-permute-done.2.refs_4_.refs_8_.refs_12_.refs_16_.refs_7_.refs_15_.refs_23_ = f32[4,9,16,128]{3,2,1,0:T(8,128)S(1)} collective-permute-done((f32[4,9,16,128]{3,2,1,0:T(8,128)S(1)}, f32[4,9,16,128]{3,2,1,0:T(8,128)S(1)}, u32[]{:S(2)}, u32[]{:S(2)}) %collective-permute-start.2) | collective-permute-done | bytes 294944 | tf_op jit(solution)/shard_map/ppermute | solution.py:35
  26.2 5.2 %prepare.1 = (bf16[1024,192]{1,0:T(8,128)(2,1)S(1)}, bf16[1024,192]{1,0:T(8,128)(2,1)S(1)}, bf16[1024,192]{1,0:T(8,128)(2,1)S(1)}, bf16[1024,192]{1,0:T(8,128)(2,1)S(1)}, f32[4,8,16,128]{3,2,1,0:T(8,128)S(1)}) custom-call(s32[1]{0:T(128)} %bitcast.me_ref, s32[16,4,2]{2,1,0:T(4,128)S(1)} %copy.5.pattern_ref, f32[16,4,32,64]{3,2,1,0:T(8,128)S(1)} %copy-done.1, ...), custom_call_target="tpu_custom_call" | custom-call | flops 1 | bytes 1 | tf_op jit(solution)/shard_map/prepare/pallas_call | solution.py:93
  31.5 6.9 %collective-permute-start = (f32[1,8,16,128]{3,2,1,0:T(8,128)S(1)}, f32[1,8,16,128]{3,2,1,0:T(8,128)S(1)}, u32[]{:S(2)}, u32[]{:S(2)}) collective-permute-start(f32[1,8,16,128]{3,2,1,0:T(8,128)S(1)} %slice.3), channel_id=1, source_target_pairs={{0,1},{1,2},{2,3},{4,5},{5,6},{6,7},{8,9},{9,10},{10,11},{12,13},{... | collective-permute-start | bytes 196616 | tf_op jit(solution)/shard_map/ppermute | solution.py:28
  38.4 15.0 %fluxes_0xyz0_1xyz0_2xyz0_3xy0.1 = (f32[9,64,128]{2,1,0:T(8,128)S(1)}, f32[9,64,128]{2,1,0:T(8,128)S(1)}, f32[9,64,128]{2,1,0:T(8,128)S(1)}, f32[9,64,128]{2,1,0...) custom-call(s32[1]{0:T(128)} %bitcast.me_ref, ...), custom_call_target="tpu_custom_call" | custom-call | bytes 1 | tf_op jit(solution)/shard_map/fluxes_0xyz0_1xyz0_2xyz0_3xy0/pallas_call | solution.py:289
  53.5 1.9 %collective-permute-start.8 = (f32[8,128,128]{2,1,0:T(8,128)S(1)}, f32[8,128,128]{2,1,0:T(8,128)S(1)}, u32[]{:S(2)}, u32[]{:S(2)}) collective-permute-start(f32[8,128,128]{2,1,0:T(8,128)S(1)} %get-tuple-element.56), channel_id=1, source_target_pairs={{0,1},{1,2},{2,3},{4,5},{5,6},{6,7},{8,9},{9,10},{10,11},{12,13},{... | collective-permute-start | bytes 1572872 | tf_op jit(solution)/shard_map/ppermute | solution.py:28
  55.5 2.6 %collective-permute-start.9 = (f32[8,128,128]{2,1,0:T(8,128)S(1)}, f32[8,128,128]{2,1,0:T(8,128)S(1)}, u32[]{:S(2)}, u32[]{:S(2)}) collective-permute-start(f32[8,128,128]{2,1,0:T(8,128)S(1)} %get-tuple-element.57), channel_id=1, source_target_pairs={{1,0},{2,1},{3,2},{5,4},{6,5},{7,6},{9,8},{10,9},{11,10},{13,12},{... | collective-permute-start | bytes 1572872 | tf_op jit(solution)/shard_map/ppermute | solution.py:28
  58.1 8.8 %fluxes_0xyz1_1xyz1_2xyz1_3xy1.1 = (f32[9,64,128]{2,1,0:T(8,128)S(1)}, f32[9,64,128]{2,1,0:T(8,128)S(1)}, f32[9,64,128]{2,1,0:T(8,128)S(1)}, f32[9,64,128]{2,1,0:T(8,128)S(1)}) custom-call(s32[1]{0:T(128)} %bitcast.me_ref, f32[4,8,16,128]{3,2,1,0:T(8,128)S(1)} %get-tuple-element.42.w_ref, bf16[1024,192]{1,0:T(8,128)(2,1)S(1)} %get-tuple-element.44.refs_0_.refs_1_, ...), custom_call_target="tpu_custom_call" | custom-call | flops 5905580032 | bytes 1 | tf_op jit(solution)/shard_map/fluxes_0xyz1_1xyz1_2xyz1_3xy1/pallas_call | solution.py:289
  66.9 3.0 %fluxes_3z0_-1z0_3z1_-1z1.1 = (f32[4,9,16,128]{3,2,1,0:T(8,128)S(1)}, f32[4,9,16,128]{3,2,1,0:T(8,128)S(1)}, f32[4,9,16,128]{3,2,1,0:T(8,128)S(1)}, f32[4,9,16,128]{3,2,1,0:T(8,128)S(1)}) custom-call(s32[1]{0:T(128)} %bitcast.me_ref, f32[4,8,16,128]{3,2,1,0:T(8,128)S(1)} %get-tuple-element.42.w_ref, bf16[1024,192]{1,0:T(8,128)(2,1)S(1)} %get-tuple-element.43.refs_1_.refs_0_, ...), custom_call_target="tpu_custom_call" | custom-call | flops 2147483648 | bytes 1 | tf_op jit(solution)/shard_map/fluxes_3z0_-1z0_3z1_-1z1/pallas_call | solution.py:289
  69.9 3.4 %collective-permute-start.10 = (f32[4,9,16,128]{3,2,1,0:T(8,128)S(1)}, f32[4,9,16,128]{3,2,1,0:T(8,128)S(1)}, u32[]{:S(2)}, u32[]{:S(2)}) collective-permute-start(f32[4,9,16,128]{3,2,1,0:T(8,128)S(1)} %get-tuple-element.66), channel_id=1, source_target_pairs={{0,28},{4,24},{8,20},{12,16},{16,12},{20,8},{24,4},{28,0},{1,29},{... | collective-permute-start | bytes 884744 | tf_op jit(solution)/shard_map/ppermute | solution.py:35
  73.3 1.8 %collective-permute-start.11 = (f32[4,9,16,128]{3,2,1,0:T(8,128)S(1)}, f32[4,9,16,128]{3,2,1,0:T(8,128)S(1)}, u32[]{:S(2)}, u32[]{:S(2)}) collective-permute-start(f32[4,9,16,128]{3,2,1,0:T(8,128)S(1)} %get-tuple-element.67), channel_id=1, source_target_pairs={{0,24},{4,28},{8,16},{12,20},{16,8},{20,12},{24,0},{28,4},{1,25},{... | collective-permute-start | bytes 884744 | tf_op jit(solution)/shard_map/ppermute | solution.py:35
  75.1 9.6 %collective-permute-start.12 = (f32[4,9,16,128]{3,2,1,0:T(8,128)S(1)}, f32[4,9,16,128]{3,2,1,0:T(8,128)S(1)}, u32[]{:S(2)}, u32[]{:S(2)}) collective-permute-start(f32[4,9,16,128]{3,2,1,0:T(8,128)S(1)} %get-tuple-element.68), channel_id=1, source_target_pairs={{0,20},{4,16},{8,28},{12,24},{16,4},{20,0},{24,12},{28,8},{1,21},{... | collective-permute-start | bytes 884744 | tf_op jit(solution)/shard_map/ppermute | solution.py:35
  84.7 11.8 %fluxes_0xyz1_1xyz1_2xyz1_3xy1_3z0_-1z0_3z1_-1z1.1 = (f32[4,9,16,128]{3,2,1,0:T(8,128)S(1)}, f32[4,9,16,128]{3,2,1,0:T(8,128)S(1)}, f32[4,9,16,128]{3,2,1,0:T(8,128)S(1)}, f32[4,9,16,128]{3,2,1,0:T(8,128)S(1)}) custom-call(s32[1]{0:T(128)} %bitcast.me_ref, f32[4,8,16,128]{3,2,1,0:T(8,128)S(1)} %get-tuple-element.42.w_ref, ...), custom_call_target="tpu_custom_call" | custom-call | flops 8053063680 | bytes 1 | tf_op jit(solution)/shard_map/fluxes_0xyz1_1xyz1_2xyz1_3xy1_3z0_-1z0_3z1_-1z1/pallas_call | solution.py:289
  96.5 1.3 collective-permute-start.14
  97.8 15.0 %collective-permute-start.15 = (f32[4,9,16,128]{3,2,1,0:T(8,128)S(1)}, f32[4,9,16,128]{3,2,1,0:T(8,128)S(1)}, u32[]{:S(2)}, u32[]{:S(2)}) collective-permute-start(f32[4,9,16,128]{3,2,1,0:T(8,128)S(1)} %get-tuple-element.76), channel_id=1, source_target_pairs={{0,8},{4,12},{8,0},{12,4},{16,24},{20,28},{24,16},{28,20},{1,9},{5... | collective-permute-start | bytes 884744 | tf_op jit(solution)/shard_map/ppermute | solution.py:35
  112.9 1.7 %collective-permute-start.16 = (f32[4,9,16,128]{3,2,1,0:T(8,128)S(1)}, f32[4,9,16,128]{3,2,1,0:T(8,128)S(1)}, u32[]{:S(2)}, u32[]{:S(2)}) collective-permute-start(f32[4,9,16,128]{3,2,1,0:T(8,128)S(1)} %get-tuple-element.77), channel_id=1, source_target_pairs={{0,4},{4,0},{8,12},{12,8},{16,20},{20,16},{24,28},{28,24},{1,5},{5... | collective-permute-start | bytes 884744 | tf_op jit(solution)/shard_map/ppermute | solution.py:35
  114.6 9.9 %collective-permute-done.12.refs_2_ = f32[4,9,16,128]{3,2,1,0:T(8,128)S(1)} collective-permute-done((f32[4,9,16,128]{3,2,1,0:T(8,128)S(1)}, f32[4,9,16,128]{3,2,1,0:T(8,128)S(1)}, u32[]{:S(2)}, u32[]{:S(2)}) %collective-permute-start.12) | collective-permute-done | bytes 294944 | tf_op jit(solution)/shard_map/ppermute | solution.py:35
  124.5 7.3 %collective-permute-done.13.refs_3_ = f32[4,9,16,128]{3,2,1,0:T(8,128)S(1)} collective-permute-done((f32[4,9,16,128]{3,2,1,0:T(8,128)S(1)}, f32[4,9,16,128]{3,2,1,0:T(8,128)S(1)}, u32[]{:S(2)}, u32[]{:S(2)}) %collective-permute-start.13) | collective-permute-done | bytes 294944 | tf_op jit(solution)/shard_map/ppermute | solution.py:35
  132.3 2.3 %unpack.1 = f32[16,4,64,128]{3,2,1,0:T(8,128)} custom-call(s32[1]{0:T(128)} %bitcast.me_ref, f32[4,9,16,128]{3,2,1,0:T(8,128)S(1)} %collective-permute-done.10.refs_0_, f32[4,9,16,128]{3,2,1,0:T(8,128)S(1)} %collective-permute-done.11.refs_1_, f32[4,9,16,128]{3,2,1,0:T(8,128)S(1)} %collective-permute-done.12.refs_2_, ...), custom_call_target="tpu_custom_call" | custom-call | flops 1 | bytes 1 | tf_op jit(solution)/shard_map/unpack/pallas_call | solution.py:335
  (28 shorter events, 4.4 us)
Async XLA Ops:
  0.0 25.1 %copy-start.3 = (s32[16,4,2]{0,2,1:T(2,128)S(1)}, s32[16,4,2]{0,2,1:T(2,128)}, u32[]{:S(2)}) copy-start(s32[16,4,2]{0,2,1:T(2,128)} %param.7) | copy-start | bytes 1540
  0.0 1.6 %copy-start = (f32[16,4,64,128]{3,2,1,0:T(8,128)S(1)}, f32[16,4,64,128]{3,2,1,0:T(8,128)}, u32[]{:S(2)}) copy-start(f32[16,4,64,128]{3,2,1,0:T(8,128)} %field_ref.3) | copy-start | bytes 6291460
  1.6 23.7 %copy-start.1 = (f32[16,4,32,64]{3,2,1,0:T(8,128)S(1)}, f32[16,4,32,64]{3,2,1,0:T(8,128)}, u32[]{:S(2)}) copy-start(f32[16,4,32,64]{3,2,1,0:T(8,128)} %blocks_ref.1) | copy-start | bytes 1572868
  3.6 8.8 %collective-permute-start.1 = (f32[4,9,16,128]{3,2,1,0:T(8,128)S(1)}, f32[4,9,16,128]{3,2,1,0:T(8,128)S(1)}, u32[]{:S(2)}, u32[]{:S(2)}) collective-permute-start(f32[4,9,16,128]{3,2,1,0:T(8,128)S(1)} %get-tuple-element.47), channel_id=1, source_target_pairs={{0,4},{4,0},{8,12},{12,8},{16,20},{20,16},{24,28},{28,24},{1,5},{5... | collective-permute-start | bytes 884744 | tf_op jit(solution)/shard_map/ppermute | solution.py:35
  5.6 19.1 %collective-permute-start.2 = (f32[4,9,16,128]{3,2,1,0:T(8,128)S(1)}, f32[4,9,16,128]{3,2,1,0:T(8,128)S(1)}, u32[]{:S(2)}, u32[]{:S(2)}) collective-permute-start(f32[4,9,16,128]{3,2,1,0:T(8,128)S(1)} %get-tuple-element.48), channel_id=1, source_target_pairs={{0,8},{4,12},{8,0},{12,4},{16,24},{20,28},{24,16},{28,20},{1,9},{5... | collective-permute-start | bytes 884744 | tf_op jit(solution)/shard_map/ppermute | solution.py:35
  6.9 24.6 %collective-permute-start.3 = (f32[4,9,16,128]{3,2,1,0:T(8,128)}, f32[4,9,16,128]{3,2,1,0:T(8,128)S(1)}, u32[]{:S(2)}, u32[]{:S(2)}) collective-permute-start(f32[4,9,16,128]{3,2,1,0:T(8,128)} %get-tuple-element.49), channel_id=1, source_target_pairs={{0,12},{4,8},{8,4},{12,0},{16,28},{20,24},{24,20},{28,16},{1,13},{... | collective-permute-start | bytes 884744 | tf_op jit(solution)/shard_map/ppermute | solution.py:35
  6.9 46.5 %collective-permute-start.4 = (f32[4,9,16,128]{3,2,1,0:T(8,128)}, f32[4,9,16,128]{3,2,1,0:T(8,128)S(1)}, u32[]{:S(2)}, u32[]{:S(2)}) collective-permute-start(f32[4,9,16,128]{3,2,1,0:T(8,128)} %get-tuple-element.52), channel_id=1, source_target_pairs={{0,16},{4,20},{8,24},{12,28},{16,0},{20,4},{24,8},{28,12},{1,17},{... | collective-permute-start | bytes 884744 | tf_op jit(solution)/shard_map/ppermute | solution.py:35
  9.3 44.1 %collective-permute-start.5 = (f32[4,9,16,128]{3,2,1,0:T(8,128)}, f32[4,9,16,128]{3,2,1,0:T(8,128)S(1)}, u32[]{:S(2)}, u32[]{:S(2)}) collective-permute-start(f32[4,9,16,128]{3,2,1,0:T(8,128)} %get-tuple-element.53), channel_id=1, source_target_pairs={{0,20},{4,16},{8,28},{12,24},{16,4},{20,0},{24,12},{28,8},{1,21},{... | collective-permute-start | bytes 884744 | tf_op jit(solution)/shard_map/ppermute | solution.py:35
  12.3 41.1 %collective-permute-start.6 = (f32[4,9,16,128]{3,2,1,0:T(8,128)}, f32[4,9,16,128]{3,2,1,0:T(8,128)S(1)}, u32[]{:S(2)}, u32[]{:S(2)}) collective-permute-start(f32[4,9,16,128]{3,2,1,0:T(8,128)} %get-tuple-element.54), channel_id=1, source_target_pairs={{0,24},{4,28},{8,16},{12,20},{16,8},{20,12},{24,0},{28,4},{1,25},{... | collective-permute-start | bytes 884744 | tf_op jit(solution)/shard_map/ppermute | solution.py:35
  24.7 28.7 %collective-permute-start.7 = (f32[4,9,16,128]{3,2,1,0:T(8,128)}, f32[4,9,16,128]{3,2,1,0:T(8,128)S(1)}, u32[]{:S(2)}, u32[]{:S(2)}) collective-permute-start(f32[4,9,16,128]{3,2,1,0:T(8,128)} %get-tuple-element.55), channel_id=1, source_target_pairs={{0,28},{4,24},{8,20},{12,16},{16,12},{20,8},{24,4},{28,0},{1,29},{... | collective-permute-start | bytes 884744 | tf_op jit(solution)/shard_map/ppermute | solution.py:35
  25.3 1.0 copy-start.2
  31.5 35.4 %collective-permute-start = (f32[1,8,16,128]{3,2,1,0:T(8,128)S(1)}, f32[1,8,16,128]{3,2,1,0:T(8,128)S(1)}, u32[]{:S(2)}, u32[]{:S(2)}) collective-permute-start(f32[1,8,16,128]{3,2,1,0:T(8,128)S(1)} %slice.3), channel_id=1, source_target_pairs={{0,1},{1,2},{2,3},{4,5},{5,6},{6,7},{8,9},{9,10},{10,11},{12,13},{... | collective-permute-start | bytes 196616 | tf_op jit(solution)/shard_map/ppermute | solution.py:28
  53.5 13.4 %collective-permute-start.8 = (f32[8,128,128]{2,1,0:T(8,128)S(1)}, f32[8,128,128]{2,1,0:T(8,128)S(1)}, u32[]{:S(2)}, u32[]{:S(2)}) collective-permute-start(f32[8,128,128]{2,1,0:T(8,128)S(1)} %get-tuple-element.56), channel_id=1, source_target_pairs={{0,1},{1,2},{2,3},{4,5},{5,6},{6,7},{8,9},{9,10},{10,11},{12,13},{... | collective-permute-start | bytes 1572872 | tf_op jit(solution)/shard_map/ppermute | solution.py:28
  55.5 11.4 %collective-permute-start.9 = (f32[8,128,128]{2,1,0:T(8,128)S(1)}, f32[8,128,128]{2,1,0:T(8,128)S(1)}, u32[]{:S(2)}, u32[]{:S(2)}) collective-permute-start(f32[8,128,128]{2,1,0:T(8,128)S(1)} %get-tuple-element.57), channel_id=1, source_target_pairs={{1,0},{2,1},{3,2},{5,4},{6,5},{7,6},{9,8},{10,9},{11,10},{13,12},{... | collective-permute-start | bytes 1572872 | tf_op jit(solution)/shard_map/ppermute | solution.py:28
  69.9 27.9 %collective-permute-start.10 = (f32[4,9,16,128]{3,2,1,0:T(8,128)S(1)}, f32[4,9,16,128]{3,2,1,0:T(8,128)S(1)}, u32[]{:S(2)}, u32[]{:S(2)}) collective-permute-start(f32[4,9,16,128]{3,2,1,0:T(8,128)S(1)} %get-tuple-element.66), channel_id=1, source_target_pairs={{0,28},{4,24},{8,20},{12,16},{16,12},{20,8},{24,4},{28,0},{1,29},{... | collective-permute-start | bytes 884744 | tf_op jit(solution)/shard_map/ppermute | solution.py:35
  73.3 39.6 %collective-permute-start.11 = (f32[4,9,16,128]{3,2,1,0:T(8,128)S(1)}, f32[4,9,16,128]{3,2,1,0:T(8,128)S(1)}, u32[]{:S(2)}, u32[]{:S(2)}) collective-permute-start(f32[4,9,16,128]{3,2,1,0:T(8,128)S(1)} %get-tuple-element.67), channel_id=1, source_target_pairs={{0,24},{4,28},{8,16},{12,20},{16,8},{20,12},{24,0},{28,4},{1,25},{... | collective-permute-start | bytes 884744 | tf_op jit(solution)/shard_map/ppermute | solution.py:35
  75.1 49.4 %collective-permute-start.12 = (f32[4,9,16,128]{3,2,1,0:T(8,128)S(1)}, f32[4,9,16,128]{3,2,1,0:T(8,128)S(1)}, u32[]{:S(2)}, u32[]{:S(2)}) collective-permute-start(f32[4,9,16,128]{3,2,1,0:T(8,128)S(1)} %get-tuple-element.68), channel_id=1, source_target_pairs={{0,20},{4,16},{8,28},{12,24},{16,4},{20,0},{24,12},{28,8},{1,21},{... | collective-permute-start | bytes 884744 | tf_op jit(solution)/shard_map/ppermute | solution.py:35
  84.7 47.1 %collective-permute-start.13 = (f32[4,9,16,128]{3,2,1,0:T(8,128)S(1)}, f32[4,9,16,128]{3,2,1,0:T(8,128)S(1)}, u32[]{:S(2)}, u32[]{:S(2)}) collective-permute-start(f32[4,9,16,128]{3,2,1,0:T(8,128)S(1)} %get-tuple-element.69), channel_id=1, source_target_pairs={{0,16},{4,20},{8,24},{12,28},{16,0},{20,4},{24,8},{28,12},{1,17},{... | collective-permute-start | bytes 884744 | tf_op jit(solution)/shard_map/ppermute | solution.py:35
  96.5 35.3 %collective-permute-start.14 = (f32[4,9,16,128]{3,2,1,0:T(8,128)S(1)}, f32[4,9,16,128]{3,2,1,0:T(8,128)S(1)}, u32[]{:S(2)}, u32[]{:S(2)}) collective-permute-start(f32[4,9,16,128]{3,2,1,0:T(8,128)S(1)} %get-tuple-element.75), channel_id=1, source_target_pairs={{0,12},{4,8},{8,4},{12,0},{16,28},{20,24},{24,20},{28,16},{1,13},{... | collective-permute-start | bytes 884744 | tf_op jit(solution)/shard_map/ppermute | solution.py:35
  97.8 34.5 %collective-permute-start.15 = (f32[4,9,16,128]{3,2,1,0:T(8,128)S(1)}, f32[4,9,16,128]{3,2,1,0:T(8,128)S(1)}, u32[]{:S(2)}, u32[]{:S(2)}) collective-permute-start(f32[4,9,16,128]{3,2,1,0:T(8,128)S(1)} %get-tuple-element.76), channel_id=1, source_target_pairs={{0,8},{4,12},{8,0},{12,4},{16,24},{20,28},{24,16},{28,20},{1,9},{5... | collective-permute-start | bytes 884744 | tf_op jit(solution)/shard_map/ppermute | solution.py:35
  112.9 19.5 %collective-permute-start.16 = (f32[4,9,16,128]{3,2,1,0:T(8,128)S(1)}, f32[4,9,16,128]{3,2,1,0:T(8,128)S(1)}, u32[]{:S(2)}, u32[]{:S(2)}) collective-permute-start(f32[4,9,16,128]{3,2,1,0:T(8,128)S(1)} %get-tuple-element.77), channel_id=1, source_target_pairs={{0,4},{4,0},{8,12},{12,8},{16,20},{20,16},{24,28},{28,24},{1,5},{5... | collective-permute-start | bytes 884744 | tf_op jit(solution)/shard_map/ppermute | solution.py:35
where the time goes:
time: 136 us; the launch traced here: 135 us
  starting transfers between devices  54.8 us (40%)
  Pallas kernels  48.1 us (35%)
  waiting for transfers between devices  28.9 us (21%)
  local copies, waits for them, and re-layouts  2.67 us (2%)
    ppermute x14, starting transfers between devices, exchange(): lax.ppermute(pieces[s], 'mode', [(i, i ^ s) for i in range(count)])  43.3 us
    pallas_call x4, Pallas kernels, fluxes(): pl.pallas_call(functools.partial(flux_kernel, count, plan), in_specs=[SME...  38.5 us
    ppermute x14, waiting for transfers between devices, exchange(): lax.ppermute(pieces[s], 'mode', [(i, i ^ s) for i in range(count)])  28.9 us
    ppermute x3, starting transfers between devices, from_behind(): lax.ppermute(value, axis, [(source, source + steps) for source in range(f...  11.4 us
    pallas_call x1, Pallas kernels, prepare(): pl.pallas_call(functools.partial(prepare_kernel, count), in_specs=[SMEM,...  5.24 us
  transfers between devices with their start and end apart: 17, of which 5 were waited for; matrix products, arithmetic and copies ran while one was open for 0% of the time, Pallas kernels for 30%

commit v1 on v0

--- a/solution.py
+++ b/solution.py
@@ -225,7 +225,7 @@
         ref[...] = sums[key][...] if key in sums else jnp.zeros_like(ref)
 
     for plane, directions, half, sides in tasks:
-        per_step = 4 if len(directions) > 1 else 8
+        per_step = 4 if len(directions) > 1 and len(dense_keys) > 1 else rows
 
         def step(i, carry, plane=plane, directions=directions, half=half, sides=sides, per_step=per_step):
             groups, weights = [], []
@@ -283,7 +283,7 @@
     number_out = len(out_shape)
     out_shape += [jax.ShapeDtypeStruct(whole, F32)] * len(carried)
     out_shape += [jax.ShapeDtypeStruct((rows, half_modes, width), F32)] * len(edges)
-    scratch = [pltpu.VMEM((len(listed),) + whole, F32), pltpu.VMEM((3 * half_modes, 12 * width), BF16)]
+    scratch = [pltpu.VMEM((len(listed),) + whole, F32), pltpu.VMEM((3 * half_modes, (12 if len(dense_keys) > 1 else 3 * rows) * width), BF16)]
     scratch += [pltpu.VMEM(whole, F32)] * len(final)
     units = rows * sum(len(directions) * len(sides) for _, directions, _, sides in tasks)
     results = pl.pallas_call(

time: 136 us -> 135 us (level)
  transfers between devices with their start and end apart: 17 -> 17, of which waited for: 5 -> 6; matrix products, arithmetic and copies ran while one was open for 0% -> 0% of each run, Pallas kernels for 30% -> 30%
where the time goes in v1:
time: 135 us; the launch traced here: 133 us
  starting transfers between devices  54.6 us (40%)
  Pallas kernels  46.9 us (35%)
  waiting for transfers between devices  29.1 us (22%)
  local copies, waits for them, and re-layouts  2.67 us (2%)
    ppermute x14, starting transfers between devices, exchange(): lax.ppermute(pieces[s], 'mode', [(i, i ^ s) for i in range(count)])  43.1 us
    pallas_call x4, Pallas kernels, fluxes(): pl.pallas_call(functools.partial(flux_kernel, count, plan), in_specs=[SME...  37.4 us
    ppermute x14, waiting for transfers between devices, exchange(): lax.ppermute(pieces[s], 'mode', [(i, i ^ s) for i in range(count)])  28.9 us
    ppermute x3, starting transfers between devices, from_behind(): lax.ppermute(value, axis, [(source, source + steps) for source in range(f...  11.4 us
    pallas_call x1, Pallas kernels, prepare(): pl.pallas_call(functools.partial(prepare_kernel, count), in_specs=[SMEM,...  5.24 us
  transfers between devices with their start and end apart: 17, of which 6 were waited for; matrix products, arithmetic and copies ran while one was open for 0% of the time, Pallas kernels for 30%

profile of v1, /device:TPU:1, one launch (start us, length us, event | category | flops | bytes accessed | tf_op | source)
XLA Modules:
  0.0 133.4 jit_solution(13568750914261439414)
XLA Ops:
  0.0 1.6 %copy-done = f32[16,4,64,128]{3,2,1,0:T(8,128)S(1)} copy-done((f32[16,4,64,128]{3,2,1,0:T(8,128)S(1)}, f32[16,4,64,128]{3,2,1,0:T(8,128)}, u32[]{:S(2)}) %copy-start) | copy-done | bytes 2097176
  1.6 1.9 %pack.1 = (f32[4,9,16,128]{3,2,1,0:T(8,128)S(1)}, f32[4,9,16,128]{3,2,1,0:T(8,128)S(1)}, f32[4,9,16,128]{3,2,1,0:T(8,128)S(1)}, f32[4,9,16,128]{3,2,1,0:T(8,128)...) custom-call(s32[1]{0:T(128)} %bitcast.me_ref, ...), custom_call_target="tpu_custom_call" | custom-call | flops 1 | bytes 1 | tf_op jit(solution)/shard_map/pack/pallas_call | solution.py:120
  3.6 2.0 %collective-permute-start.1 = (f32[4,9,16,128]{3,2,1,0:T(8,128)S(1)}, f32[4,9,16,128]{3,2,1,0:T(8,128)S(1)}, u32[]{:S(2)}, u32[]{:S(2)}) collective-permute-start(f32[4,9,16,128]{3,2,1,0:T(8,128)S(1)} %get-tuple-element.47), channel_id=1, source_target_pairs={{0,4},{4,0},{8,12},{12,8},{16,20},{20,16},{24,28},{28,24},{1,5},{5... | collective-permute-start | bytes 884744 | tf_op jit(solution)/shard_map/ppermute | solution.py:35
  6.9 2.4 %collective-permute-start.4 = (f32[4,9,16,128]{3,2,1,0:T(8,128)}, f32[4,9,16,128]{3,2,1,0:T(8,128)S(1)}, u32[]{:S(2)}, u32[]{:S(2)}) collective-permute-start(f32[4,9,16,128]{3,2,1,0:T(8,128)} %get-tuple-element.52), channel_id=1, source_target_pairs={{0,16},{4,20},{8,24},{12,28},{16,0},{20,4},{24,8},{28,12},{1,17},{... | collective-permute-start | bytes 884744 | tf_op jit(solution)/shard_map/ppermute | solution.py:35
  10.3 2.0 %collective-permute-done.1.refs_3_.refs_7_.refs_11_.refs_15_.refs_6_.refs_14_.refs_22_ = f32[4,9,16,128]{3,2,1,0:T(8,128)S(1)} collective-permute-done((f32[4,9,16,128]{3,2,1,0:T(8,128)S(1)}, f32[4,9,16,128]{3,2,1,0:T(8,128)S(1)}, u32[]{:S(2)}, u32[]{:S(2)}) %collective-permute-start.1) | collective-permute-done | bytes 294944 | tf_op jit(solution)/shard_map/ppermute | solution.py:35
  12.3 3.3 %collective-permute-start.6 = (f32[4,9,16,128]{3,2,1,0:T(8,128)}, f32[4,9,16,128]{3,2,1,0:T(8,128)S(1)}, u32[]{:S(2)}, u32[]{:S(2)}) collective-permute-start(f32[4,9,16,128]{3,2,1,0:T(8,128)} %get-tuple-element.54), channel_id=1, source_target_pairs={{0,24},{4,28},{8,16},{12,20},{16,8},{20,12},{24,0},{28,4},{1,25},{... | collective-permute-start | bytes 884744 | tf_op jit(solution)/shard_map/ppermute | solution.py:35
  15.6 9.1 %collective-permute-done.2.refs_4_.refs_8_.refs_12_.refs_16_.refs_7_.refs_15_.refs_23_ = f32[4,9,16,128]{3,2,1,0:T(8,128)S(1)} collective-permute-done((f32[4,9,16,128]{3,2,1,0:T(8,128)S(1)}, f32[4,9,16,128]{3,2,1,0:T(8,128)S(1)}, u32[]{:S(2)}, u32[]{:S(2)}) %collective-permute-start.2) | collective-permute-done | bytes 294944 | tf_op jit(solution)/shard_map/ppermute | solution.py:35
  26.2 5.2 %prepare.1 = (bf16[1024,192]{1,0:T(8,128)(2,1)S(1)}, bf16[1024,192]{1,0:T(8,128)(2,1)S(1)}, bf16[1024,192]{1,0:T(8,128)(2,1)S(1)}, bf16[1024,192]{1,0:T(8,128)(2,1)S(1)}, f32[4,8,16,128]{3,2,1,0:T(8,128)S(1)}) custom-call(s32[1]{0:T(128)} %bitcast.me_ref, s32[16,4,2]{2,1,0:T(4,128)S(1)} %copy.5.pattern_ref, f32[16,4,32,64]{3,2,1,0:T(8,128)S(1)} %copy-done.1, ...), custom_call_target="tpu_custom_call" | custom-call | flops 1 | bytes 1 | tf_op jit(solution)/shard_map/prepare/pallas_call | solution.py:93
  31.5 6.9 %collective-permute-start = (f32[1,8,16,128]{3,2,1,0:T(8,128)S(1)}, f32[1,8,16,128]{3,2,1,0:T(8,128)S(1)}, u32[]{:S(2)}, u32[]{:S(2)}) collective-permute-start(f32[1,8,16,128]{3,2,1,0:T(8,128)S(1)} %slice.3), channel_id=1, source_target_pairs={{0,1},{1,2},{2,3},{4,5},{5,6},{6,7},{8,9},{9,10},{10,11},{12,13},{... | collective-permute-start | bytes 196616 | tf_op jit(solution)/shard_map/ppermute | solution.py:28
  38.4 15.0 %fluxes_0xyz0_1xyz0_2xyz0_3xy0.1 = (f32[9,64,128]{2,1,0:T(8,128)S(1)}, f32[9,64,128]{2,1,0:T(8,128)S(1)}, f32[9,64,128]{2,1,0:T(8,128)S(1)}, f32[9,64,128]{2,1,0...) custom-call(s32[1]{0:T(128)} %bitcast.me_ref, ...), custom_call_target="tpu_custom_call" | custom-call | bytes 1 | tf_op jit(solution)/shard_map/fluxes_0xyz0_1xyz0_2xyz0_3xy0/pallas_call | solution.py:289
  53.5 1.9 %collective-permute-start.8 = (f32[8,128,128]{2,1,0:T(8,128)S(1)}, f32[8,128,128]{2,1,0:T(8,128)S(1)}, u32[]{:S(2)}, u32[]{:S(2)}) collective-permute-start(f32[8,128,128]{2,1,0:T(8,128)S(1)} %get-tuple-element.56), channel_id=1, source_target_pairs={{0,1},{1,2},{2,3},{4,5},{5,6},{6,7},{8,9},{9,10},{10,11},{12,13},{... | collective-permute-start | bytes 1572872 | tf_op jit(solution)/shard_map/ppermute | solution.py:28
  55.5 2.6 %collective-permute-start.9 = (f32[8,128,128]{2,1,0:T(8,128)S(1)}, f32[8,128,128]{2,1,0:T(8,128)S(1)}, u32[]{:S(2)}, u32[]{:S(2)}) collective-permute-start(f32[8,128,128]{2,1,0:T(8,128)S(1)} %get-tuple-element.57), channel_id=1, source_target_pairs={{1,0},{2,1},{3,2},{5,4},{6,5},{7,6},{9,8},{10,9},{11,10},{13,12},{... | collective-permute-start | bytes 1572872 | tf_op jit(solution)/shard_map/ppermute | solution.py:28
  58.1 7.6 %fluxes_0xyz1_1xyz1_2xyz1_3xy1.1 = (f32[9,64,128]{2,1,0:T(8,128)S(1)}, f32[9,64,128]{2,1,0:T(8,128)S(1)}, f32[9,64,128]{2,1,0:T(8,128)S(1)}, f32[9,64,128]{2,1,0:T(8,128)S(1)}) custom-call(s32[1]{0:T(128)} %bitcast.me_ref, f32[4,8,16,128]{3,2,1,0:T(8,128)S(1)} %get-tuple-element.42.w_ref, bf16[1024,192]{1,0:T(8,128)(2,1)S(1)} %get-tuple-element.44.refs_0_.refs_1_, ...), custom_call_target="tpu_custom_call" | custom-call | flops 5905580032 | bytes 1 | tf_op jit(solution)/shard_map/fluxes_0xyz1_1xyz1_2xyz1_3xy1/pallas_call | solution.py:289
  66.0 3.0 %fluxes_3z0_-1z0_3z1_-1z1.1 = (f32[4,9,16,128]{3,2,1,0:T(8,128)S(1)}, f32[4,9,16,128]{3,2,1,0:T(8,128)S(1)}, f32[4,9,16,128]{3,2,1,0:T(8,128)S(1)}, f32[4,9,16,128]{3,2,1,0:T(8,128)S(1)}) custom-call(s32[1]{0:T(128)} %bitcast.me_ref, f32[4,8,16,128]{3,2,1,0:T(8,128)S(1)} %get-tuple-element.42.w_ref, bf16[1024,192]{1,0:T(8,128)(2,1)S(1)} %get-tuple-element.43.refs_1_.refs_0_, ...), custom_call_target="tpu_custom_call" | custom-call | flops 2147483648 | bytes 1 | tf_op jit(solution)/shard_map/fluxes_3z0_-1z0_3z1_-1z1/pallas_call | solution.py:289
  68.9 3.4 %collective-permute-start.10 = (f32[4,9,16,128]{3,2,1,0:T(8,128)S(1)}, f32[4,9,16,128]{3,2,1,0:T(8,128)S(1)}, u32[]{:S(2)}, u32[]{:S(2)}) collective-permute-start(f32[4,9,16,128]{3,2,1,0:T(8,128)S(1)} %get-tuple-element.66), channel_id=1, source_target_pairs={{0,28},{4,24},{8,20},{12,16},{16,12},{20,8},{24,4},{28,0},{1,29},{... | collective-permute-start | bytes 884744 | tf_op jit(solution)/shard_map/ppermute | solution.py:35
  72.3 1.8 %collective-permute-start.11 = (f32[4,9,16,128]{3,2,1,0:T(8,128)S(1)}, f32[4,9,16,128]{3,2,1,0:T(8,128)S(1)}, u32[]{:S(2)}, u32[]{:S(2)}) collective-permute-start(f32[4,9,16,128]{3,2,1,0:T(8,128)S(1)} %get-tuple-element.67), channel_id=1, source_target_pairs={{0,24},{4,28},{8,16},{12,20},{16,8},{20,12},{24,0},{28,4},{1,25},{... | collective-permute-start | bytes 884744 | tf_op jit(solution)/shard_map/ppermute | solution.py:35
  74.1 10.1 %collective-permute-start.12 = (f32[4,9,16,128]{3,2,1,0:T(8,128)S(1)}, f32[4,9,16,128]{3,2,1,0:T(8,128)S(1)}, u32[]{:S(2)}, u32[]{:S(2)}) collective-permute-start(f32[4,9,16,128]{3,2,1,0:T(8,128)S(1)} %get-tuple-element.68), channel_id=1, source_target_pairs={{0,20},{4,16},{8,28},{12,24},{16,4},{20,0},{24,12},{28,8},{1,21},{... | collective-permute-start | bytes 884744 | tf_op jit(solution)/shard_map/ppermute | solution.py:35
  84.2 11.8 %fluxes_0xyz1_1xyz1_2xyz1_3xy1_3z0_-1z0_3z1_-1z1.1 = (f32[4,9,16,128]{3,2,1,0:T(8,128)S(1)}, f32[4,9,16,128]{3,2,1,0:T(8,128)S(1)}, f32[4,9,16,128]{3,2,1,0:T(8,128)S(1)}, f32[4,9,16,128]{3,2,1,0:T(8,128)S(1)}) custom-call(s32[1]{0:T(128)} %bitcast.me_ref, f32[4,8,16,128]{3,2,1,0:T(8,128)S(1)} %get-tuple-element.42.w_ref, ...), custom_call_target="tpu_custom_call" | custom-call | flops 8053063680 | bytes 1 | tf_op jit(solution)/shard_map/fluxes_0xyz1_1xyz1_2xyz1_3xy1_3z0_-1z0_3z1_-1z1/pallas_call | solution.py:289
  96.0 1.3 collective-permute-start.14
  97.4 14.4 %collective-permute-start.15 = (f32[4,9,16,128]{3,2,1,0:T(8,128)S(1)}, f32[4,9,16,128]{3,2,1,0:T(8,128)S(1)}, u32[]{:S(2)}, u32[]{:S(2)}) collective-permute-start(f32[4,9,16,128]{3,2,1,0:T(8,128)S(1)} %get-tuple-element.76), channel_id=1, source_target_pairs={{0,8},{4,12},{8,0},{12,4},{16,24},{20,28},{24,16},{28,20},{1,9},{5... | collective-permute-start | bytes 884744 | tf_op jit(solution)/shard_map/ppermute | solution.py:35
  111.7 1.7 %collective-permute-start.16 = (f32[4,9,16,128]{3,2,1,0:T(8,128)S(1)}, f32[4,9,16,128]{3,2,1,0:T(8,128)S(1)}, u32[]{:S(2)}, u32[]{:S(2)}) collective-permute-start(f32[4,9,16,128]{3,2,1,0:T(8,128)S(1)} %get-tuple-element.77), channel_id=1, source_target_pairs={{0,4},{4,0},{8,12},{12,8},{16,20},{20,16},{24,28},{28,24},{1,5},{5... | collective-permute-start | bytes 884744 | tf_op jit(solution)/shard_map/ppermute | solution.py:35
  113.4 9.9 %collective-permute-done.12.refs_2_ = f32[4,9,16,128]{3,2,1,0:T(8,128)S(1)} collective-permute-done((f32[4,9,16,128]{3,2,1,0:T(8,128)S(1)}, f32[4,9,16,128]{3,2,1,0:T(8,128)S(1)}, u32[]{:S(2)}, u32[]{:S(2)}) %collective-permute-start.12) | collective-permute-done | bytes 294944 | tf_op jit(solution)/shard_map/ppermute | solution.py:35
  123.3 7.3 %collective-permute-done.13.refs_3_ = f32[4,9,16,128]{3,2,1,0:T(8,128)S(1)} collective-permute-done((f32[4,9,16,128]{3,2,1,0:T(8,128)S(1)}, f32[4,9,16,128]{3,2,1,0:T(8,128)S(1)}, u32[]{:S(2)}, u32[]{:S(2)}) %collective-permute-start.13) | collective-permute-done | bytes 294944 | tf_op jit(solution)/shard_map/ppermute | solution.py:35
  131.2 2.3 %unpack.1 = f32[16,4,64,128]{3,2,1,0:T(8,128)} custom-call(s32[1]{0:T(128)} %bitcast.me_ref, f32[4,9,16,128]{3,2,1,0:T(8,128)S(1)} %collective-permute-done.10.refs_0_, f32[4,9,16,128]{3,2,1,0:T(8,128)S(1)} %collective-permute-done.11.refs_1_, f32[4,9,16,128]{3,2,1,0:T(8,128)S(1)} %collective-permute-done.12.refs_2_, ...), custom_call_target="tpu_custom_call" | custom-call | flops 1 | bytes 1 | tf_op jit(solution)/shard_map/unpack/pallas_call | solution.py:335
  (28 shorter events, 4.6 us)
Async XLA Ops:
  0.0 25.1 %copy-start.3 = (s32[16,4,2]{0,2,1:T(2,128)S(1)}, s32[16,4,2]{0,2,1:T(2,128)}, u32[]{:S(2)}) copy-start(s32[16,4,2]{0,2,1:T(2,128)} %param.7) | copy-start | bytes 1540
  0.0 1.6 %copy-start = (f32[16,4,64,128]{3,2,1,0:T(8,128)S(1)}, f32[16,4,64,128]{3,2,1,0:T(8,128)}, u32[]{:S(2)}) copy-start(f32[16,4,64,128]{3,2,1,0:T(8,128)} %field_ref.3) | copy-start | bytes 6291460
  1.6 23.7 %copy-start.1 = (f32[16,4,32,64]{3,2,1,0:T(8,128)S(1)}, f32[16,4,32,64]{3,2,1,0:T(8,128)}, u32[]{:S(2)}) copy-start(f32[16,4,32,64]{3,2,1,0:T(8,128)} %blocks_ref.1) | copy-start | bytes 1572868
  3.6 8.8 %collective-permute-start.1 = (f32[4,9,16,128]{3,2,1,0:T(8,128)S(1)}, f32[4,9,16,128]{3,2,1,0:T(8,128)S(1)}, u32[]{:S(2)}, u32[]{:S(2)}) collective-permute-start(f32[4,9,16,128]{3,2,1,0:T(8,128)S(1)} %get-tuple-element.47), channel_id=1, source_target_pairs={{0,4},{4,0},{8,12},{12,8},{16,20},{20,16},{24,28},{28,24},{1,5},{5... | collective-permute-start | bytes 884744 | tf_op jit(solution)/shard_map/ppermute | solution.py:35
  5.6 19.1 %collective-permute-start.2 = (f32[4,9,16,128]{3,2,1,0:T(8,128)S(1)}, f32[4,9,16,128]{3,2,1,0:T(8,128)S(1)}, u32[]{:S(2)}, u32[]{:S(2)}) collective-permute-start(f32[4,9,16,128]{3,2,1,0:T(8,128)S(1)} %get-tuple-element.48), channel_id=1, source_target_pairs={{0,8},{4,12},{8,0},{12,4},{16,24},{20,28},{24,16},{28,20},{1,9},{5... | collective-permute-start | bytes 884744 | tf_op jit(solution)/shard_map/ppermute | solution.py:35
  6.9 24.6 %collective-permute-start.3 = (f32[4,9,16,128]{3,2,1,0:T(8,128)}, f32[4,9,16,128]{3,2,1,0:T(8,128)S(1)}, u32[]{:S(2)}, u32[]{:S(2)}) collective-permute-start(f32[4,9,16,128]{3,2,1,0:T(8,128)} %get-tuple-element.49), channel_id=1, source_target_pairs={{0,12},{4,8},{8,4},{12,0},{16,28},{20,24},{24,20},{28,16},{1,13},{... | collective-permute-start | bytes 884744 | tf_op jit(solution)/shard_map/ppermute | solution.py:35
  6.9 46.5 %collective-permute-start.4 = (f32[4,9,16,128]{3,2,1,0:T(8,128)}, f32[4,9,16,128]{3,2,1,0:T(8,128)S(1)}, u32[]{:S(2)}, u32[]{:S(2)}) collective-permute-start(f32[4,9,16,128]{3,2,1,0:T(8,128)} %get-tuple-element.52), channel_id=1, source_target_pairs={{0,16},{4,20},{8,24},{12,28},{16,0},{20,4},{24,8},{28,12},{1,17},{... | collective-permute-start | bytes 884744 | tf_op jit(solution)/shard_map/ppermute | solution.py:35
  9.3 44.1 %collective-permute-start.5 = (f32[4,9,16,128]{3,2,1,0:T(8,128)}, f32[4,9,16,128]{3,2,1,0:T(8,128)S(1)}, u32[]{:S(2)}, u32[]{:S(2)}) collective-permute-start(f32[4,9,16,128]{3,2,1,0:T(8,128)} %get-tuple-element.53), channel_id=1, source_target_pairs={{0,20},{4,16},{8,28},{12,24},{16,4},{20,0},{24,12},{28,8},{1,21},{... | collective-permute-start | bytes 884744 | tf_op jit(solution)/shard_map/ppermute | solution.py:35
  12.3 41.1 %collective-permute-start.6 = (f32[4,9,16,128]{3,2,1,0:T(8,128)}, f32[4,9,16,128]{3,2,1,0:T(8,128)S(1)}, u32[]{:S(2)}, u32[]{:S(2)}) collective-permute-start(f32[4,9,16,128]{3,2,1,0:T(8,128)} %get-tuple-element.54), channel_id=1, source_target_pairs={{0,24},{4,28},{8,16},{12,20},{16,8},{20,12},{24,0},{28,4},{1,25},{... | collective-permute-start | bytes 884744 | tf_op jit(solution)/shard_map/ppermute | solution.py:35
  24.7 28.7 %collective-permute-start.7 = (f32[4,9,16,128]{3,2,1,0:T(8,128)}, f32[4,9,16,128]{3,2,1,0:T(8,128)S(1)}, u32[]{:S(2)}, u32[]{:S(2)}) collective-permute-start(f32[4,9,16,128]{3,2,1,0:T(8,128)} %get-tuple-element.55), channel_id=1, source_target_pairs={{0,28},{4,24},{8,20},{12,16},{16,12},{20,8},{24,4},{28,0},{1,29},{... | collective-permute-start | bytes 884744 | tf_op jit(solution)/shard_map/ppermute | solution.py:35
  25.3 1.0 copy-start.2
  31.5 34.2 %collective-permute-start = (f32[1,8,16,128]{3,2,1,0:T(8,128)S(1)}, f32[1,8,16,128]{3,2,1,0:T(8,128)S(1)}, u32[]{:S(2)}, u32[]{:S(2)}) collective-permute-start(f32[1,8,16,128]{3,2,1,0:T(8,128)S(1)} %slice.3), channel_id=1, source_target_pairs={{0,1},{1,2},{2,3},{4,5},{5,6},{6,7},{8,9},{9,10},{10,11},{12,13},{... | collective-permute-start | bytes 196616 | tf_op jit(solution)/shard_map/ppermute | solution.py:28
  53.5 12.2 %collective-permute-start.8 = (f32[8,128,128]{2,1,0:T(8,128)S(1)}, f32[8,128,128]{2,1,0:T(8,128)S(1)}, u32[]{:S(2)}, u32[]{:S(2)}) collective-permute-start(f32[8,128,128]{2,1,0:T(8,128)S(1)} %get-tuple-element.56), channel_id=1, source_target_pairs={{0,1},{1,2},{2,3},{4,5},{5,6},{6,7},{8,9},{9,10},{10,11},{12,13},{... | collective-permute-start | bytes 1572872 | tf_op jit(solution)/shard_map/ppermute | solution.py:28
  55.5 10.5 %collective-permute-start.9 = (f32[8,128,128]{2,1,0:T(8,128)S(1)}, f32[8,128,128]{2,1,0:T(8,128)S(1)}, u32[]{:S(2)}, u32[]{:S(2)}) collective-permute-start(f32[8,128,128]{2,1,0:T(8,128)S(1)} %get-tuple-element.57), channel_id=1, source_target_pairs={{1,0},{2,1},{3,2},{5,4},{6,5},{7,6},{9,8},{10,9},{11,10},{13,12},{... | collective-permute-start | bytes 1572872 | tf_op jit(solution)/shard_map/ppermute | solution.py:28
  68.9 28.4 %collective-permute-start.10 = (f32[4,9,16,128]{3,2,1,0:T(8,128)S(1)}, f32[4,9,16,128]{3,2,1,0:T(8,128)S(1)}, u32[]{:S(2)}, u32[]{:S(2)}) collective-permute-start(f32[4,9,16,128]{3,2,1,0:T(8,128)S(1)} %get-tuple-element.66), channel_id=1, source_target_pairs={{0,28},{4,24},{8,20},{12,16},{16,12},{20,8},{24,4},{28,0},{1,29},{... | collective-permute-start | bytes 884744 | tf_op jit(solution)/shard_map/ppermute | solution.py:35
  72.3 39.4 %collective-permute-start.11 = (f32[4,9,16,128]{3,2,1,0:T(8,128)S(1)}, f32[4,9,16,128]{3,2,1,0:T(8,128)S(1)}, u32[]{:S(2)}, u32[]{:S(2)}) collective-permute-start(f32[4,9,16,128]{3,2,1,0:T(8,128)S(1)} %get-tuple-element.67), channel_id=1, source_target_pairs={{0,24},{4,28},{8,16},{12,20},{16,8},{20,12},{24,0},{28,4},{1,25},{... | collective-permute-start | bytes 884744 | tf_op jit(solution)/shard_map/ppermute | solution.py:35
  74.1 49.2 %collective-permute-start.12 = (f32[4,9,16,128]{3,2,1,0:T(8,128)S(1)}, f32[4,9,16,128]{3,2,1,0:T(8,128)S(1)}, u32[]{:S(2)}, u32[]{:S(2)}) collective-permute-start(f32[4,9,16,128]{3,2,1,0:T(8,128)S(1)} %get-tuple-element.68), channel_id=1, source_target_pairs={{0,20},{4,16},{8,28},{12,24},{16,4},{20,0},{24,12},{28,8},{1,21},{... | collective-permute-start | bytes 884744 | tf_op jit(solution)/shard_map/ppermute | solution.py:35
  84.2 46.4 %collective-permute-start.13 = (f32[4,9,16,128]{3,2,1,0:T(8,128)S(1)}, f32[4,9,16,128]{3,2,1,0:T(8,128)S(1)}, u32[]{:S(2)}, u32[]{:S(2)}) collective-permute-start(f32[4,9,16,128]{3,2,1,0:T(8,128)S(1)} %get-tuple-element.69), channel_id=1, source_target_pairs={{0,16},{4,20},{8,24},{12,28},{16,0},{20,4},{24,8},{28,12},{1,17},{... | collective-permute-start | bytes 884744 | tf_op jit(solution)/shard_map/ppermute | solution.py:35
  96.0 34.6 %collective-permute-start.14 = (f32[4,9,16,128]{3,2,1,0:T(8,128)S(1)}, f32[4,9,16,128]{3,2,1,0:T(8,128)S(1)}, u32[]{:S(2)}, u32[]{:S(2)}) collective-permute-start(f32[4,9,16,128]{3,2,1,0:T(8,128)S(1)} %get-tuple-element.75), channel_id=1, source_target_pairs={{0,12},{4,8},{8,4},{12,0},{16,28},{20,24},{24,20},{28,16},{1,13},{... | collective-permute-start | bytes 884744 | tf_op jit(solution)/shard_map/ppermute | solution.py:35
  97.4 33.8 %collective-permute-start.15 = (f32[4,9,16,128]{3,2,1,0:T(8,128)S(1)}, f32[4,9,16,128]{3,2,1,0:T(8,128)S(1)}, u32[]{:S(2)}, u32[]{:S(2)}) collective-permute-start(f32[4,9,16,128]{3,2,1,0:T(8,128)S(1)} %get-tuple-element.76), channel_id=1, source_target_pairs={{0,8},{4,12},{8,0},{12,4},{16,24},{20,28},{24,16},{28,20},{1,9},{5... | collective-permute-start | bytes 884744 | tf_op jit(solution)/shard_map/ppermute | solution.py:35
  111.7 19.5 %collective-permute-start.16 = (f32[4,9,16,128]{3,2,1,0:T(8,128)S(1)}, f32[4,9,16,128]{3,2,1,0:T(8,128)S(1)}, u32[]{:S(2)}, u32[]{:S(2)}) collective-permute-start(f32[4,9,16,128]{3,2,1,0:T(8,128)S(1)} %get-tuple-element.77), channel_id=1, source_target_pairs={{0,4},{4,0},{8,12},{12,8},{16,20},{20,16},{24,28},{28,24},{1,5},{5... | collective-permute-start | bytes 884744 | tf_op jit(solution)/shard_map/ppermute | solution.py:35
